TPU v7x, 32 devices: a whole 2x2x4 slice. The times are simulated.
32 devices in a mesh: groups: 2 (over x), pool: 8 (over z, y), tensor: 2 (over core).
Axes of the slice: x: 2, y: 2, z: 4, core: 2. Of those that a mesh axis runs over, the one named last changes fastest.
Arguments:
- queries: bfloat16 [16, 64, 3584], P(('groups', 'pool'), None, 'tensor'), parts along dimension 0, may hold values from -10 to 10
- new_kv: bfloat16 [16, 2, 64, 3584], P(('groups', 'pool'), None, None, 'tensor'), parts along dimension 0, may hold values from -10 to 10
- kv_pool: bfloat16 [128, 2, 32, 3584], P(('groups', 'pool'), None, None, 'tensor'), parts along dimension 0, may hold values from -10 to 10
- block_table: int32 [16, 8], P(('groups', 'pool')), parts along dimension 0, may hold values from -1 to 63, as said below
- prefix_len: int32 [16], P(('groups', 'pool')), parts along dimension 0, may hold values from 1 to 256, as said below
- out_weight: bfloat16 [3584, 7168], P('tensor', 'pool'), may hold values from -0.59765625 to 0.59765625
Outputs:
- projected: bfloat16 [1024, 7168], P(('groups', 'tensor'), 'pool'), parts along dimension 0
There are 2 independent parts, one for each index of `groups`. A program takes and returns all parts, laid end to end along the dimension named above; an argument that names none is the same for every part. Nothing has to cross between parts.
Inputs may be any that keep to these rules, and one draw needn't show every extreme that they name: `block_table`: conversation v's first k entries are slots and the rest -1, k = ceil(prefix_len[v] / 32); no slot is named twice; the entries of one conversation lie in distinct blocks of 8 slots (distinct pool indices). `prefix_len`: some conversation has exactly 256 cached tokens.
All inputs are finite; a program needn't handle non-finite values.
Results may differ from a plain program's by a relative error of at most 0.0049.
Values may be sent and summed in bfloat16 or wider, within the bound.
A program may use at most 128 MiB of HBM per device.

v0:
```python
import jax
import jax.numpy as jnp
from jax import lax
from jax.sharding import PartitionSpec as P

ALL_HEADS = 64
HEAD_DIM = 112
HEADS = 32


masked_fill = -1e30


def alibi_slopes(head_first, head_count):
    order = (head_first + jnp.arange(head_count, dtype=jnp.int32) + 1).astype(jnp.float32)
    return jnp.exp2(-8.0 * order / ALL_HEADS)


def block_stats(query, keys, values, query_pos, key_pos, key_limit, slopes, score_scale):
    heads = slopes.shape[0]
    query_heads = query.reshape(query.shape[0], heads, -1)
    key_heads = keys.reshape(keys.shape[0], keys.shape[1], heads, -1)
    value_heads = values.reshape(values.shape[0], values.shape[1], heads, -1)
    raw_scores = jnp.einsum(
        "qhd,bkhd->bhqk", query_heads, key_heads, preferred_element_type=jnp.float32
    )
    distance = (query_pos[None, None, :, None] - key_pos[:, None, None, :]).astype(jnp.float32)
    scores = raw_scores * score_scale - slopes[None, :, None, None] * distance
    usable = (key_pos[:, None, None, :] < key_limit[:, None, None, None]) & (
        key_pos[:, None, None, :] <= query_pos[None, None, :, None]
    )
    masked = jnp.where(usable, scores, masked_fill)
    block_max = jnp.max(masked, axis=3)
    weights = jnp.where(usable, jnp.exp(masked - block_max[..., None]), 0.0).astype(jnp.bfloat16)
    block_sum = jnp.sum(weights.astype(jnp.float32), axis=3)
    block_acc = jnp.einsum(
        "bhqk,bkhd->bqhd", weights, value_heads, preferred_element_type=jnp.float32
    )
    return (block_max, block_sum, block_acc)


def combine_blocks(block_max, block_sum, block_acc):
    overall = jnp.max(block_max, axis=0)
    factor = jnp.exp(block_max - overall[None])
    denom = jnp.sum(block_sum * factor, axis=0)
    numer = jnp.sum(block_acc * jnp.transpose(factor, (0, 2, 1))[..., None], axis=0)
    context = numer / jnp.transpose(denom)[..., None]
    return context.reshape(context.shape[0], -1).astype(jnp.bfloat16)


def on_device(queries, new_kv, kv_pool, block_table, prefix_len, out_weight):
    owners = lax.axis_size("pool")
    slot_count = kv_pool.shape[0]
    block_len = kv_pool.shape[2]
    head_cols = queries.shape[2]
    new_count = queries.shape[1]
    heads_here = head_cols // HEAD_DIM
    head_first = ALL_HEADS - HEADS + lax.axis_index("tensor") * heads_here
    slopes = alibi_slopes(head_first, heads_here)
    score_scale = HEAD_DIM ** (-0.5)
    length = prefix_len[0]
    own_query = queries[0]
    query_pos = length + jnp.arange(new_count, dtype=jnp.int32)
    table_row = block_table[0]
    owner_of = jnp.where(table_row >= 0, table_row // slot_count, -1)
    matched = (owner_of[:, None] == jnp.arange(owners, dtype=jnp.int32)[None, :]).astype(jnp.int32)
    want_slot = jnp.sum(matched * (table_row % slot_count + 1)[:, None], axis=0) - 1
    want_pos = (
        jnp.sum(matched * (jnp.arange(table_row.shape[0], dtype=jnp.int32) + 1)[:, None], axis=0)
        - 1
    )
    request = jnp.stack([want_slot, want_pos, jnp.full((owners,), length, jnp.int32)], axis=1)
    requests = lax.all_to_all(request, "pool", split_axis=0, concat_axis=0, tiled=True)
    has_block = requests[:, 0] >= 0
    stored = jnp.where(
        has_block[:, None, None, None],
        kv_pool[jnp.where(has_block, requests[:, 0], 0)],
        jnp.zeros((), jnp.bfloat16),
    )
    near = block_stats(
        own_query,
        new_kv[0, 0][None],
        new_kv[0, 1][None],
        query_pos,
        query_pos[None],
        (length + new_count)[None],
        slopes,
        score_scale,
    )
    every_query = lax.all_gather(queries, "pool", axis=0, tiled=True)

    def owner_side(other_query, other_blocks, asked):
        is_live = asked[0] >= 0
        other_pos = asked[2] + jnp.arange(new_count, dtype=jnp.int32)
        key_pos = (jnp.maximum(asked[1], 0) * block_len + jnp.arange(block_len, dtype=jnp.int32))[
            None
        ]
        key_limit = jnp.where(is_live, asked[2], 0)[None]
        return block_stats(
            other_query,
            other_blocks[0][None],
            other_blocks[1][None],
            other_pos,
            key_pos,
            key_limit,
            slopes,
            score_scale,
        )

    far_max, far_sum, far_acc = jax.vmap(owner_side)(every_query, stored, requests)
    far_acc = far_acc.reshape(owners, new_count, head_cols)
    far_max, far_sum, far_acc = (
        lax.all_to_all(far_max[:, 0], "pool", split_axis=0, concat_axis=0, tiled=True),
        lax.all_to_all(far_sum[:, 0], "pool", split_axis=0, concat_axis=0, tiled=True),
        lax.all_to_all(far_acc, "pool", split_axis=0, concat_axis=0, tiled=True),
    )
    far = (far_max, far_sum, far_acc.reshape(owners, new_count, heads_here, HEAD_DIM))
    joined = tuple(
        (
            jnp.concatenate([first_part, second_part], axis=0)
            for first_part, second_part in zip(far, near)
        )
    )
    context = combine_blocks(*joined)
    flat_rows = lax.all_gather(context[None], "pool", axis=0, tiled=True).reshape(-1, head_cols)
    terms = jnp.dot(flat_rows, out_weight, preferred_element_type=jnp.float32)
    summed = lax.psum_scatter(terms, "tensor", scatter_dimension=0, tiled=True)
    return summed.astype(jnp.bfloat16)


def solution(mesh):
    placed = (
        P(("groups", "pool"), None, "tensor"),
        P(("groups", "pool"), None, None, "tensor"),
        P(("groups", "pool"), None, None, "tensor"),
        P(("groups", "pool"), None),
        P(("groups", "pool")),
        P("tensor", "pool"),
    )
    return jax.shard_map(
        on_device,
        mesh=mesh,
        in_specs=placed,
        out_specs=P(("groups", "tensor"), "pool"),
        check_vma=False,
    )
```

profile of v0, /device:TPU:0, one launch (start us, length us, event | category | flops | bytes accessed | tf_op | source)
XLA Modules:
  0.0 260.3 jit_solution(10912595297586992283)
XLA Ops:
  9.7 7.3 %all-to-all-start = ((s32[8,1,3]{2,1,0:T(1,128)}), s32[8,1,3]{2,1,0:T(1,128)S(1)}, u32[]{:S(2)}, u32[]{:S(2)}) async-start(s32[8,1,3]{2,1,0:T(1,128)} %copy.34), calls=%async_computation | async-start | bytes 8192 | tf_op jit(solution)/shard_map/all_to_all | solution.py:73
  17.0 6.4 %all-to-all-done = s32[8,1,3]{2,1,0:T(1,128)S(1)} async-done(((s32[8,1,3]{2,1,0:T(1,128)}), s32[8,1,3]{2,1,0:T(1,128)S(1)}, u32[]{:S(2)}, u32[]{:S(2)}) %all-to-all-start) | async-done | bytes 128 | tf_op jit(solution)/shard_map/all_to_all | solution.py:73
  23.5 3.4 %gather_fusion = bf16[8,2,32,1792]{3,2,1,0:T(8,128)(2,1)} fusion(bf16[8,2,32,1792]{3,2,1,0:T(8,128)(2,1)} %param.8, s32[1024]{0:T(1024)S(1)} %pad_clamp_fusion), kind=kCustom, calls=%fused_computation | custom fusion | bytes 3670048 | tf_op jit(solution)/shard_map/gather | solution.py:77
  29.9 3.6 %reshape.403 = bf16[8,32,16,112]{3,2,1,0:T(8,128)(2,1)} reshape(bf16[8,1,32,1792]{3,2,1,0:T(8,128)(2,1)} %get-tuple-element.7) | data formatting | bytes 1835008 | tf_op jit(solution)/shard_map/reshape.11
  33.5 3.6 %reshape.402 = bf16[8,32,16,112]{3,2,1,0:T(8,128)(2,1)} reshape(bf16[8,1,32,1792]{3,2,1,0:T(8,128)(2,1)} %get-tuple-element.8) | data formatting | bytes 1835008 | tf_op jit(solution)/shard_map/reshape.18
  37.6 20.9 %all-gather.3.cloned.1.call-done = bf16[8,64,1792]{2,1,0:T(8,128)(2,1)} async-done(((bf16[1,64,1792]{2,1,0:T(8,128)(2,1)}), bf16[8,64,1792]{2,1,0:T(8,128)(2,1)}) %all-gather.3.cloned.1.call-update) | async-done | bytes 1835024 | tf_op jit(solution)/shard_map/all_gather | solution.py:90
  58.6 5.5 %reshape.404 = bf16[8,64,16,112]{3,2,1,0:T(8,128)(2,1)} reshape(bf16[8,64,1792]{2,1,0:T(8,128)(2,1)} %all-gather.3.cloned.1.call-done) | data formatting | bytes 3670016 | tf_op jit(solution)/shard_map/vmap()/reshape | solution.py:21
  64.0 4.5 %fusion.26 = (f32[8,16,64]{2,1,0:T(8,128)S(1)}, f32[8,1,16,64,32]{3,4,2,0,1:T(8,128)}) fusion(f32[8,64,32]{1,2,0:T(8,128)S(1)} %subtract_convert_fusion, f32[16]{0:T(128)S(1)} %multiply_exponential_fusion, bf16[8,64,16,112]{3,2,1,0:T(8,128)(2,1)} %reshape.404, bf16[8,32,16,112]{3,2,1,0:T(8,128)(2,1)} %reshape.403, pred[8,64,32]{1,2,0:T(8,128)(4,1)S(1)} %compare_and_fusion), kind=kOutput, calls=%fused_computation.69 | convolution fusion | flops 60022784 | bytes 3915840 | tf_op jit(solution)/shard_map/vmap(qhd,bkhd->bhqk)/dot_general | solution.py:24
  69.2 3.6 %all-to-all-start.2 = ((f32[8,1,1024]{2,1,0:T(1,128)}), f32[8,1,1024]{2,1,0:T(1,128)S(1)}, u32[]{:S(2)}, u32[]{:S(2)}) async-start(f32[8,1,1024]{2,1,0:T(1,128)} %reshape.421), calls=%async_computation.2 | async-start | bytes 65536 | tf_op jit(solution)/shard_map/all_to_all | solution.py:113
  72.9 2.2 convert_reduce_fusion
  75.8 3.7 %all-to-all-done.2 = f32[8,1,1024]{2,1,0:T(1,128)S(1)} async-done(((f32[8,1,1024]{2,1,0:T(1,128)}), f32[8,1,1024]{2,1,0:T(1,128)S(1)}, u32[]{:S(2)}, u32[]{:S(2)}) %all-to-all-start.2) | async-done | bytes 32800 | tf_op jit(solution)/shard_map/all_to_all | solution.py:113
  79.6 3.5 %all-to-all-start.3 = ((f32[8,1,1024]{2,1,0:T(1,128)}), f32[8,1,1024]{2,1,0:T(1,128)S(1)}, u32[]{:S(2)}, u32[]{:S(2)}) async-start(f32[8,1,1024]{2,1,0:T(1,128)} %reshape.423), calls=%async_computation.3 | async-start | bytes 65536 | tf_op jit(solution)/shard_map/all_to_all | solution.py:114
  83.1 2.8 %convolution_bitcast_fusion = f32[8,1,64,16,112]{4,2,3,0,1:T(8,128)S(1)} fusion(bf16[8,32,16,112]{3,2,1,0:T(8,128)(2,1)} %reshape.402, f32[8,1,16,64,32]{3,4,2,0,1:T(8,128)} %get-tuple-element.21, f32[8,16,64]{2,1,0:T(8,128)S(1)} %get-tuple-element.20, pred[8,64,32]{1,2,0:T(8,128)(4,1)S(1)} %compare_and_fusion), kind=kOutput, calls=%fused_computation.3 | convolution fusion | flops 59506688 | bytes 5685248 | tf_op jit(solution)/shard_map/vmap(bhqk,bkhd->bqhd)/dot_general | solution.py:36
  85.9 4.3 %copy.39 = f32[8,1,64,16,112]{4,3,2,0,1:T(8,128)} copy(f32[8,1,64,16,112]{4,2,3,0,1:T(8,128)S(1)} %convolution_bitcast_fusion) | data formatting | bytes 7340032 | tf_op jit(solution)/shard_map/vmap(bhqk,bkhd->bqhd)/transpose | solution.py:36
  90.2 5.6 %reshape.406 = f32[8,64,1792]{2,1,0:T(8,128)} reshape(f32[8,1,64,16,112]{4,3,2,0,1:T(8,128)} %copy.39) | data formatting | bytes 7340032 | tf_op jit(solution)/shard_map/reshape | solution.py:111
  95.7 5.9 %all-to-all-start.1 = ((f32[8,64,1792]{2,1,0:T(8,128)}), f32[8,64,1792]{2,1,0:T(8,128)}, u32[]{:S(2)}, u32[]{:S(2)}) async-start(f32[8,64,1792]{2,1,0:T(8,128)} %reshape.406), calls=%async_computation.1 | async-start | bytes 7340032 | tf_op jit(solution)/shard_map/all_to_all | solution.py:115
  102.8 1.8 fusion.24
  113.8 68.1 %all-to-all-done.1 = f32[8,64,1792]{2,1,0:T(8,128)} async-done(((f32[8,64,1792]{2,1,0:T(8,128)}), f32[8,64,1792]{2,1,0:T(8,128)}, u32[]{:S(2)}, u32[]{:S(2)}) %all-to-all-start.1) | async-done | bytes 3670048 | tf_op jit(solution)/shard_map/all_to_all | solution.py:115
  181.9 5.8 %reshape.407 = f32[8,64,16,112]{3,2,1,0:T(8,128)} reshape(f32[8,64,1792]{2,1,0:T(8,128)} %all-to-all-done.1) | data formatting | bytes 7340032 | tf_op jit(solution)/shard_map/reshape | solution.py:117
  187.8 4.0 %fusion = f32[64,16,112]{2,1,0:T(8,128)S(1)} fusion(f32[1,64,16,112]{3,2,1,0:T(8,128)} %copy.44, f32[8,64,16,112]{3,2,1,0:T(8,128)} %reshape.407, f32[9,64,16]{2,1,0:T(8,128)S(1)} %copy.45), kind=kLoop, calls=%fused_computation.2 | loop fusion | flops 2981888 | bytes 4624384 | tf_op jit(solution)/shard_map/reduce_sum | solution.py:46
  193.0 45.4 %all-gather.5.cloned.1.call-done = bf16[8,64,1792]{2,1,0:T(8,128)(2,1)} async-done(((bf16[1,64,1792]{2,1,0:T(8,128)(2,1)}), bf16[8,64,1792]{2,1,0:T(8,128)(2,1)}) %all-gather.5.cloned.1.call-update) | async-done | bytes 1835024 | tf_op jit(solution)/shard_map/all_gather | solution.py:125
  238.4 4.8 %fusion.27 = f32[512,896]{1,0:T(8,128)} fusion(bf16[512,1792]{1,0:T(8,128)(2,1)} %bitcast.94, bf16[1792,896]{1,0:T(8,128)(2,1)S(1)} %copy-done), kind=kOutput, calls=%fused_computation.70 | convolution fusion | flops 1644167168 | bytes 6881280 | tf_op jit(solution)/shard_map/dot_general | solution.py:126
  243.2 8.6 %reduce-scatter.2.cloned.1.call-done = f32[256,896]{1,0:T(8,128)} async-done(((f32[512,896]{1,0:T(8,128)}), f32[256,896]{1,0:T(8,128)}) %reduce-scatter.2.cloned.1.call-update) | async-done | bytes 917520 | tf_op jit(solution)/shard_map/reduce_scatter | solution.py:127
  251.8 2.0 convert_element_type.65
  (56 shorter events, 18.9 us)
Async XLA Ops:
  6.5 231.8 %copy-start = (bf16[1792,896]{1,0:T(8,128)(2,1)S(1)}, bf16[1792,896]{1,0:T(8,128)(2,1)}, u32[]{:S(2)}) copy-start(bf16[1792,896]{1,0:T(8,128)(2,1)} %param.11) | copy-start | bytes 9633796
  6.5 52.0 %all-gather.3.cloned.1.call-start = ((), (), s32[]{:S(2)}) async-start(), calls=%async_computation.5 | async-start | bytes 2064384 | tf_op jit(solution)/shard_map/all_gather | solution.py:90
  9.7 13.7 %all-to-all-start = ((s32[8,1,3]{2,1,0:T(1,128)}), s32[8,1,3]{2,1,0:T(1,128)S(1)}, u32[]{:S(2)}, u32[]{:S(2)}) async-start(s32[8,1,3]{2,1,0:T(1,128)} %copy.34), calls=%async_computation | async-start | bytes 8192 | tf_op jit(solution)/shard_map/all_to_all | solution.py:73
  69.2 10.3 %all-to-all-start.2 = ((f32[8,1,1024]{2,1,0:T(1,128)}), f32[8,1,1024]{2,1,0:T(1,128)S(1)}, u32[]{:S(2)}, u32[]{:S(2)}) async-start(f32[8,1,1024]{2,1,0:T(1,128)} %reshape.421), calls=%async_computation.2 | async-start | bytes 65536 | tf_op jit(solution)/shard_map/all_to_all | solution.py:113
  79.6 16.2 %all-to-all-start.3 = ((f32[8,1,1024]{2,1,0:T(1,128)}), f32[8,1,1024]{2,1,0:T(1,128)S(1)}, u32[]{:S(2)}, u32[]{:S(2)}) async-start(f32[8,1,1024]{2,1,0:T(1,128)} %reshape.423), calls=%async_computation.3 | async-start | bytes 65536 | tf_op jit(solution)/shard_map/all_to_all | solution.py:114
  95.7 5.9 %copy-start.1 = (bf16[1,64,1792]{2,1,0:T(8,128)(2,1)S(1)}, bf16[1,64,1792]{2,1,0:T(8,128)(2,1)}, u32[]{:S(2)}) copy-start(bf16[1,64,1792]{2,1,0:T(8,128)(2,1)} %param.6) | copy-start | bytes 688132
  95.7 86.2 %all-to-all-start.1 = ((f32[8,64,1792]{2,1,0:T(8,128)}), f32[8,64,1792]{2,1,0:T(8,128)}, u32[]{:S(2)}, u32[]{:S(2)}) async-start(f32[8,64,1792]{2,1,0:T(8,128)} %reshape.406), calls=%async_computation.1 | async-start | bytes 7340032 | tf_op jit(solution)/shard_map/all_to_all | solution.py:115
  101.6 136.8 %all-gather.5.cloned.1.call-start = ((), (), s32[]{:S(2)}) async-start(), calls=%async_computation.6 | async-start | bytes 2064384 | tf_op jit(solution)/shard_map/all_gather | solution.py:125
  192.9 58.8 %reduce-scatter.2.cloned.1.call-start = ((), (), s32[]{:S(2)}) async-start(), calls=%async_computation.7 | async-start | bytes 2752512 | tf_op jit(solution)/shard_map/reduce_scatter | solution.py:127
Sparse Core Ops, SparseCore 0:
  9.5 48.9 all-gather.2
  193.1 45.2 all-gather.4
  243.3 8.3 reduce-scatter.1
where the time goes:
time: 261 us; the launch traced here: 260 us
  waiting for transfers between devices  154 us (59%)
  local copies, waits for them, and re-layouts  44.4 us (17%)
  starting transfers between devices  20.4 us (8%)
  between operations  14.2 us (5%)
  other arithmetic  13.8 us (5%)
  matrix products  13.7 us (5%)
    all_to_all x1, waiting for transfers between devices, on_device(): lax.all_to_all(far_acc, 'pool', split_axis=0, concat_axis=0, tiled=True)  68.1 us
    all_gather x1, waiting for transfers between devices, on_device(): lax.all_gather(context[None], 'pool', axis=0, tiled=True)  45.4 us
    all_gather x1, waiting for transfers between devices, on_device(): every_query = lax.all_gather(queries, 'pool', axis=0, tiled=True)  20.9 us
    another operation x4, local copies, waits for them, and re-layouts  9.57 us
    reduce_scatter x1, waiting for transfers between devices, on_device(): summed = lax.psum_scatter(terms, 'tensor', scatter_dimension=0, tiled=True)  8.56 us
    all_to_all x1, starting transfers between devices, on_device(): lax.all_to_all(request, 'pool', split_axis=0, concat_axis=0, tiled=True)  7.28 us
    all_to_all x1, waiting for transfers between devices, on_device(): lax.all_to_all(request, 'pool', split_axis=0, concat_axis=0, tiled=True)  6.38 us
    all_to_all x1, starting transfers between devices, on_device(): lax.all_to_all(far_acc, 'pool', split_axis=0, concat_axis=0, tiled=True)  5.88 us
  transfers between devices with their start and end apart: 7, of which 6 were waited for; matrix products, arithmetic and copies ran while one was open for 17% of the time, Pallas kernels for 0%

commit v1 on v0

v1 whole, which is shorter than its diff:
```python
import functools

import jax
import jax.numpy as jnp
from jax import lax
from jax.experimental import pallas as pl
from jax.experimental.pallas import tpu as pltpu
from jax.sharding import PartitionSpec as P

ALL_HEADS = 64
HEAD_DIM = 112
HEADS = 32
LANES = 128
HEAD_GROUP = 8
CHUNK = HEAD_GROUP * HEAD_DIM
CHUNK_TILES = CHUNK // LANES

masked_fill = -1e30
far_away = 1 << 30
MESH = pl.DeviceIdType.MESH


def head_window(head):
    first = head * HEAD_DIM // LANES
    last = (head * HEAD_DIM + HEAD_DIM - 1) // LANES
    return first * LANES, (last - first + 1) * LANES


def kernel(
    owners, tensors, zigzag,
    table_s, length_s, table_v, q_ref, new_ref, pool_ref, w_hbm,
    out_ref,
    tbl_send, tbl_recv, tbl_smem, k_send, v_send, k_recv, v_recv,
    p_far, p_near, inv_sum, ctx, w_ref, kept, partial_send, partial_recv,
    tbl_ss, tbl_rs, k_ss, k_rs, v_ss, v_rs, ring_ss, ring_rs, part_ss, part_rs, local_sem,
):
    n = owners
    hops = n // 2
    half = n // tensors
    me = lax.axis_index("pool")
    core = lax.axis_index("tensor")
    slots = pool_ref.shape[0]
    block_len = pool_ref.shape[2]
    new_count = q_ref.shape[1]
    max_blocks = table_v.shape[1]
    chunks = q_ref.shape[2] // CHUNK
    heads_here = chunks * HEAD_GROUP
    keys = n * block_len

    w_copy = pltpu.make_async_copy(w_hbm, w_ref, local_sem.at[0])
    w_copy.start()

    barrier = pltpu.get_barrier_semaphore()
    peers = [lax.rem(me + off, n) for off in range(1, n)]
    other_core = lax.rem(core + 1, tensors)
    for d in peers:
        pl.semaphore_signal(barrier, inc=1, device_id={"pool": d}, device_id_type=MESH)
    pl.semaphore_signal(barrier, inc=1, device_id={"tensor": other_core}, device_id_type=MESH)

    tbl_send[...] = jnp.zeros_like(tbl_send)
    tbl_send[0:1, 0:max_blocks] = table_v[...]
    pl.semaphore_wait(barrier, n)

    def table_copy(d, s):
        return pltpu.make_async_remote_copy(
            src_ref=tbl_send, dst_ref=tbl_recv.at[s],
            send_sem=tbl_ss.at[d], recv_sem=tbl_rs.at[s],
            device_id={"pool": d}, device_id_type=MESH)

    for d in peers:
        table_copy(d, me).start()
    tbl_recv[me] = tbl_send[...]
    for d in peers:
        table_copy(d, d).wait_recv()
    to_smem = pltpu.make_async_copy(tbl_recv, tbl_smem, local_sem.at[1])
    to_smem.start()
    to_smem.wait()

    def wanted_slot(d):
        def step(j, slot):
            entry = tbl_smem[d, 0, j]
            hit = (entry >= 0) & (lax.div(entry, slots) == me)
            return jnp.where(hit, lax.rem(entry, slots), slot)
        slot = jnp.int32(0)
        if max_blocks <= 8:
            for j in range(max_blocks):
                slot = step(j, slot)
            return slot
        return lax.fori_loop(0, max_blocks, step, slot)

    def key_copy(d, s):
        return pltpu.make_async_remote_copy(
            src_ref=k_send.at[d], dst_ref=k_recv.at[s],
            send_sem=k_ss.at[d], recv_sem=k_rs.at[s],
            device_id={"pool": d}, device_id_type=MESH)

    def value_copy(c, d, s):
        return pltpu.make_async_remote_copy(
            src_ref=v_send.at[c, d], dst_ref=v_recv.at[c, s],
            send_sem=v_ss.at[c, d], recv_sem=v_rs.at[c, s],
            device_id={"pool": d}, device_id_type=MESH)

    wanted = [wanted_slot(d) for d in peers]
    for d, slot in zip(peers, wanted):
        k_send[d] = pool_ref[slot, 0]
        key_copy(d, me).start()
    for c in range(chunks):
        for d, slot in zip(peers, wanted):
            v_send[c, d] = pool_ref[slot, 1, :, c * CHUNK:(c + 1) * CHUNK]
            value_copy(c, d, me).start()
    own = wanted_slot(me)
    k_recv[me] = pool_ref[own, 0]
    for c in range(chunks):
        v_recv[c, me] = pool_ref[own, 1, :, c * CHUNK:(c + 1) * CHUNK]

    length = length_s[0]
    lane = lax.broadcasted_iota(jnp.int32, (new_count, keys), 1)
    row = lax.broadcasted_iota(jnp.int32, (new_count, keys), 0)
    source = lane // block_len
    offset = lane - source * block_len
    key_pos = jnp.full((new_count, keys), far_away, jnp.int32)
    for j in range(max_blocks):
        entry = table_s[0, j]
        owner = jnp.where(entry >= 0, lax.div(entry, slots), -1)
        key_pos = jnp.where(source == owner, j * block_len + offset, key_pos)
    far_ok = key_pos < length
    far_dist = (length + row - key_pos).astype(jnp.float32)
    near_row = lax.broadcasted_iota(jnp.int32, (new_count, new_count), 0)
    near_lane = lax.broadcasted_iota(jnp.int32, (new_count, new_count), 1)
    near_ok = near_lane <= near_row
    near_dist = (near_row - near_lane).astype(jnp.float32)
    score_scale = HEAD_DIM ** -0.5

    for d in peers:
        key_copy(d, d).wait_recv()

    contract_lanes = (((1,), (1,)), ((), ()))
    for c in range(chunks):
        for h in range(HEAD_GROUP):
            head = c * HEAD_GROUP + h
            first, width = head_window(h)
            window = slice(c * CHUNK + first, c * CHUNK + first + width)
            slope = jnp.float32(0)
            for t in range(tensors):
                order = ALL_HEADS - HEADS + t * heads_here + head + 1
                slope = jnp.where(core == t, jnp.float32(2.0 ** (-8.0 * order / ALL_HEADS)), slope)
            q_lane = lax.broadcasted_iota(jnp.int32, (new_count, width), 1) + first
            inside = (q_lane >= h * HEAD_DIM) & (q_lane < (h + 1) * HEAD_DIM)
            query = jnp.where(inside, q_ref[0, :, window].astype(jnp.float32), 0.0).astype(jnp.bfloat16)
            far_keys = k_recv[:, :, window].reshape(keys, width)
            far = lax.dot_general(query, far_keys, contract_lanes, preferred_element_type=jnp.float32)
            near = lax.dot_general(query, new_ref[0, 0, :, window], contract_lanes, preferred_element_type=jnp.float32)
            far = jnp.where(far_ok, far * score_scale - slope * far_dist, masked_fill)
            near = jnp.where(near_ok, near * score_scale - slope * near_dist, masked_fill)
            top = jnp.maximum(jnp.max(far, axis=1, keepdims=True), jnp.max(near, axis=1, keepdims=True))
            far = jnp.where(far_ok, jnp.exp(far - top), 0.0).astype(jnp.bfloat16)
            near = jnp.where(near_ok, jnp.exp(near - top), 0.0).astype(jnp.bfloat16)
            total = (jnp.sum(far.astype(jnp.float32), axis=1, keepdims=True)
                     + jnp.sum(near.astype(jnp.float32), axis=1, keepdims=True))
            p_far[head] = far
            p_near[head] = near
            inv_sum[head] = jnp.broadcast_to(1.0 / total, (new_count, LANES))

    def index_at(place):
        if not zigzag:
            return place
        return jnp.where(place < hops, 2 * place, 2 * (n - 1 - place) + 1)

    if zigzag:
        parity = lax.rem(me, 2)
        place = jnp.where(parity == 0, me // 2, n - 1 - me // 2)
    else:
        place = me

    def at_distance(k):
        return index_at(lax.rem(place + k + n, n))

    right, left = at_distance(1), at_distance(-1)

    def travels(way, c, k):
        return k < hops or (k == hops and c % 2 == way)

    def ring_copy(way, c, k, block):
        return pltpu.make_async_remote_copy(
            src_ref=ctx.at[block, c], dst_ref=ctx.at[block, c],
            send_sem=ring_ss.at[way, c, k - 1], recv_sem=ring_rs.at[way, c, k - 1],
            device_id={"pool": left if way else right}, device_id_type=MESH)

    for c in range(chunks):
        for d in peers:
            value_copy(c, d, d).wait_recv()
        before = None
        tiles = []
        for h in range(HEAD_GROUP):
            head = c * HEAD_GROUP + h
            first, width = head_window(h)
            far_values = v_recv[c, :, :, first:first + width].reshape(keys, width)
            near_values = new_ref[0, 1, :, c * CHUNK + first:c * CHUNK + first + width]
            acc = (jnp.dot(p_far[head], far_values, preferred_element_type=jnp.float32)
                   + jnp.dot(p_near[head], near_values, preferred_element_type=jnp.float32))
            scale = inv_sum[head]
            begin = acc[:, :LANES] * scale
            if before is not None:
                bound = h * HEAD_DIM - first
                tile_lane = lax.broadcasted_iota(jnp.int32, (new_count, LANES), 1)
                tiles.append(jnp.where(tile_lane < bound, before, begin))
            before = begin if width == LANES else acc[:, LANES:] * scale
        for i, tile in enumerate(tiles):
            ctx[me, c, :, i * LANES:(i + 1) * LANES] = tile.astype(jnp.bfloat16)
        for way in range(2):
            if travels(way, c, 1):
                ring_copy(way, c, 1, me).start()

    w_copy.wait()

    def partial_copy(i):
        return pltpu.make_async_remote_copy(
            src_ref=partial_send.at[i], dst_ref=partial_recv.at[i],
            send_sem=part_ss.at[i], recv_sem=part_rs.at[i],
            device_id={"tensor": other_core}, device_id_type=MESH)

    def hand_on(conv, value):
        part, i = conv // half, lax.rem(conv, half)

        @pl.when(part == core)
        def _():
            kept[i] = value

        @pl.when(part != core)
        def _():
            partial_send[i] = value.astype(jnp.bfloat16)
            partial_copy(i).start()

    for k in range(hops + 1):
        origins = [me] if k == 0 else [at_distance(-k), at_distance(k)]
        blocks = origins[:1] if k == hops else origins
        value = None
        for c in range(chunks):
            if k:
                for way in range(2):
                    if travels(way, c, k):
                        ring_copy(way, c, k, origins[way]).wait_recv()
                        if travels(way, c, k + 1):
                            ring_copy(way, c, k + 1, origins[way]).start()
            rows = [ctx[b, c] for b in blocks]
            rows = rows[0] if len(rows) == 1 else jnp.concatenate(rows, axis=0)
            term = jnp.dot(rows, w_ref[c * CHUNK:(c + 1) * CHUNK, :], preferred_element_type=jnp.float32)
            value = term if value is None else value + term
        for i, b in enumerate(blocks):
            hand_on(b, value[i * new_count:(i + 1) * new_count])

    for i in range(half):
        partial_copy(i).wait_recv()
        out_ref[i * new_count:(i + 1) * new_count, :] = (
            kept[i] + partial_recv[i].astype(jnp.float32)).astype(jnp.bfloat16)

    for d in peers:
        table_copy(d, me).wait_send()
        key_copy(d, me).wait_send()
        for c in range(chunks):
            value_copy(c, d, me).wait_send()
    for k in range(1, hops + 1):
        for c in range(chunks):
            for way in range(2):
                if travels(way, c, k):
                    ring_copy(way, c, k, me).wait_send()
    for i in range(half):
        partial_copy(i).wait_send()


def on_device(owners, tensors, queries, new_kv, kv_pool, block_table, prefix_len, out_weight):
    n = owners
    new_count, head_cols = queries.shape[1:]
    block_len = kv_pool.shape[2]
    columns = out_weight.shape[1]
    chunks = head_cols // CHUNK
    heads_here = chunks * HEAD_GROUP
    half = n // tensors
    hops = n // 2
    bf16, f32 = jnp.bfloat16, jnp.float32
    vmem = pl.BlockSpec(memory_space=pltpu.VMEM)
    smem = pl.BlockSpec(memory_space=pltpu.SMEM)
    dma = pltpu.SemaphoreType.DMA
    return pl.pallas_call(
        functools.partial(kernel, owners, tensors, owners <= 8),
        out_shape=jax.ShapeDtypeStruct((half * new_count, columns), bf16),
        in_specs=[smem, smem, vmem, vmem, vmem, vmem, pl.BlockSpec(memory_space=pl.ANY)],
        out_specs=vmem,
        scratch_shapes=[
            pltpu.VMEM((8, LANES), jnp.int32),
            pltpu.VMEM((n, 8, LANES), jnp.int32),
            pltpu.SMEM((n, 8, LANES), jnp.int32),
            pltpu.VMEM((n, block_len, head_cols), bf16),
            pltpu.VMEM((chunks, n, block_len, CHUNK), bf16),
            pltpu.VMEM((n, block_len, head_cols), bf16),
            pltpu.VMEM((chunks, n, block_len, CHUNK), bf16),
            pltpu.VMEM((heads_here, new_count, n * block_len), bf16),
            pltpu.VMEM((heads_here, new_count, new_count), bf16),
            pltpu.VMEM((heads_here, new_count, LANES), f32),
            pltpu.VMEM((n, chunks, new_count, CHUNK), bf16),
            pltpu.VMEM((head_cols, columns), bf16),
            pltpu.VMEM((half, new_count, columns), f32),
            pltpu.VMEM((half, new_count, columns), bf16),
            pltpu.VMEM((half, new_count, columns), bf16),
            dma((n,)), dma((n,)), dma((n,)), dma((n,)),
            dma((chunks, n)), dma((chunks, n)),
            dma((2, chunks, hops)), dma((2, chunks, hops)),
            dma((half,)), dma((half,)), dma((2,)),
        ],
        compiler_params=pltpu.CompilerParams(
            collective_id=0, has_side_effects=True, vmem_limit_bytes=60 << 20),
    )(block_table, prefix_len, block_table, queries, new_kv, kv_pool, out_weight)


def solution(mesh):
    placed = (
        P(("groups", "pool"), None, "tensor"),
        P(("groups", "pool"), None, None, "tensor"),
        P(("groups", "pool"), None, None, "tensor"),
        P(("groups", "pool"), None),
        P(("groups", "pool")),
        P("tensor", "pool"),
    )
    return jax.shard_map(
        functools.partial(on_device, mesh.shape["pool"], mesh.shape["tensor"]),
        mesh=mesh,
        in_specs=placed,
        out_specs=P(("groups", "tensor"), "pool"),
        check_vma=False,
    )
```

time: 261 us -> 78.5 us (0.30)
  waiting for transfers between devices: 154 us -> 0 us
  Pallas kernels: 0 us -> 75.8 us
  local copies, waits for them, and re-layouts: 44.4 us -> 1.82 us
  starting transfers between devices: 20.4 us -> 0 us
  other arithmetic: 13.8 us -> 0 us
  matrix products: 13.7 us -> 0 us
  between operations: 14.2 us -> 0.66 us
    all_to_all x4 -> x0, waiting for transfers between devices: 78.2 us -> none  [the longest x1 68.1 us: on_device(): lax.all_to_all(far_acc, 'pool', split_axis=0, concat_axis=0, tiled=True)]
    pallas_call x0 -> x1, Pallas kernels: none -> 75.8 us  [on_device(): pl.pallas_call(functools.partial(kernel, owners, tensors, owners <= 8), o...]
    all_gather x2 -> x0, waiting for transfers between devices: 66.3 us -> none  [the longest x1 45.4 us: on_device(): lax.all_gather(context[None], 'pool', axis=0, tiled=True)]
    all_to_all x4 -> x0, starting transfers between devices: 20.3 us -> none  [the longest x1 7.28 us: on_device(): lax.all_to_all(request, 'pool', split_axis=0, concat_axis=0, tiled=True)]
    reshape x3 -> x0, local copies, waits for them, and re-layouts: 16.9 us -> none  [the longest x1 5.84 us: on_device(): far_acc.reshape(owners, new_count, heads_here, HEAD_DIM)]
    dot_general x5 -> x0, matrix products: 13.7 us -> none  [the longest x2 5.8 us: block_stats(): jnp.einsum('qhd,bkhd->bhqk', query_heads, key_heads, preferred_element_ty...]
    another operation x6 -> x0, local copies, waits for them, and re-layouts: 10.7 us -> none
    reduce_scatter x1 -> x0, waiting for transfers between devices: 8.56 us -> none  [on_device(): summed = lax.psum_scatter(terms, 'tensor', scatter_dimension=0, tiled=True)]
  transfers between devices with their start and end apart: 7 -> 0, of which waited for: 6 -> 0; matrix products, arithmetic and copies ran while one was open for 17% -> 0% of each run, Pallas kernels for 0% -> 0%
where the time goes in v1:
time: 78.5 us; the launch traced here: 78.3 us
  Pallas kernels  75.8 us (97%)
  local copies, waits for them, and re-layouts  1.82 us (2%)
    pallas_call x1, Pallas kernels, on_device(): pl.pallas_call(functools.partial(kernel, owners, tensors, owners <= 8), o...  75.8 us
    unnamed x1, local copies, waits for them, and re-layouts  1.82 us

profile of v1, /device:TPU:0, one launch (start us, length us, event | category | flops | bytes accessed | tf_op | source)
XLA Modules:
  0.0 78.3 jit_solution(1438709806765452246)
XLA Ops:
  0.7 75.8 %shard_map.64 = bf16[256,896]{1,0:T(8,128)(2,1)} custom-call(s32[1,8]{1,0:T(1,128)} %table_v.1, s32[1]{0:T(128)S(6)} %copy.8.length_s, s32[1,8]{1,0:T(1,128)} %table_v.1, bf16[1,64,1792]{2,1,0:T(8,128)(2,1)} %q_ref.1, bf16[1,2,64,1792]{3,2,1,0:T(8,128)(2,1)} %new_ref.1, bf16[8,2,32,1792]{3,2,1,0:T(8,128)(2,1)} %pool_ref.1, bf16[1792,896]{1,0:T(8,128)(2,1)} %w_hbm.1), custom_call_target="tpu_custom_call" | custom-call | tf_op jit(solution)/shard_map/pallas_call | solution.py:284
  76.5 1.8 %copy.9 = bf16[256,896]{1,0:T(8,128)(2,1)} copy(bf16[256,896]{1,0:T(8,128)(2,1)} %shard_map.64) | data formatting | bytes 917504

commit v2 on v1

v2 whole, which is shorter than its diff:
```python
import functools

import jax
import jax.numpy as jnp
from jax import lax
from jax.experimental import pallas as pl
from jax.experimental.pallas import tpu as pltpu
from jax.sharding import PartitionSpec as P

ALL_HEADS = 64
HEAD_DIM = 112
HEADS = 32
LANES = 128
HEAD_GROUP = 8
CHUNK = HEAD_GROUP * HEAD_DIM
CHUNK_TILES = CHUNK // LANES

masked_fill = -1e30
far_away = 1 << 30
MESH = pl.DeviceIdType.MESH


def head_window(head):
    first = head * HEAD_DIM // LANES
    last = (head * HEAD_DIM + HEAD_DIM - 1) // LANES
    return first * LANES, (last - first + 1) * LANES


def kernel(
    owners, tensors, depth,
    table_s, length_s, table_v, q_hbm, new_hbm, pool_hbm, w_hbm,
    out_ref,
    q_ref, new_ref, pool_ref, w_ref,
    tbl_send, tbl_recv, tbl_smem, k_send, v_send, k_recv, v_recv,
    p_far, p_near, inv_sum, ctx, kept, away, partial_send, partial_recv,
    tbl_ss, tbl_rs, k_ss, k_rs, v_ss, v_rs, line_ss, line_rs, side_ss, side_rs,
    part_ss, part_rs, local_sem,
):
    n = owners
    line = n // depth
    half = n // tensors
    me = lax.axis_index("pool")
    core = lax.axis_index("tensor")
    place = me // depth
    side = lax.rem(me, depth)
    slots = pool_ref.shape[0]
    block_len = pool_ref.shape[2]
    new_count = q_ref.shape[1]
    max_blocks = table_v.shape[1]
    chunks = q_ref.shape[2] // CHUNK
    heads_here = chunks * HEAD_GROUP
    keys = n * block_len

    loads = [pltpu.make_async_copy(src, dst, local_sem.at[i + 1]) for i, (src, dst) in enumerate(
        ((pool_hbm, pool_ref), (q_hbm, q_ref), (new_hbm, new_ref), (w_hbm, w_ref)))]
    for load in loads:
        load.start()

    barrier = pltpu.get_barrier_semaphore()
    peers = [lax.rem(me + off, n) for off in range(1, n)]
    other_core = lax.rem(core + 1, tensors)
    for d in peers:
        pl.semaphore_signal(barrier, inc=1, device_id={"pool": d}, device_id_type=MESH)
    pl.semaphore_signal(barrier, inc=1, device_id={"tensor": other_core}, device_id_type=MESH)

    tbl_send[...] = jnp.zeros_like(tbl_send)
    tbl_send[0:1, 0:max_blocks] = table_v[...]
    pl.semaphore_wait(barrier, n)

    def table_copy(d, s):
        return pltpu.make_async_remote_copy(
            src_ref=tbl_send, dst_ref=tbl_recv.at[s],
            send_sem=tbl_ss.at[d], recv_sem=tbl_rs.at[s],
            device_id={"pool": d}, device_id_type=MESH)

    for d in peers:
        table_copy(d, me).start()
    tbl_recv[me] = tbl_send[...]

    length = length_s[0]
    lane = lax.broadcasted_iota(jnp.int32, (new_count, keys), 1)
    row = lax.broadcasted_iota(jnp.int32, (new_count, keys), 0)
    source = lane // block_len
    offset = lane - source * block_len
    key_pos = jnp.full((new_count, keys), far_away, jnp.int32)
    for j in range(max_blocks):
        entry = table_s[0, j]
        owner = jnp.where(entry >= 0, lax.div(entry, slots), -1)
        key_pos = jnp.where(source == owner, j * block_len + offset, key_pos)
    far_ok = key_pos < length
    far_dist = (length + row - key_pos).astype(jnp.float32)
    near_row = lax.broadcasted_iota(jnp.int32, (new_count, new_count), 0)
    near_lane = lax.broadcasted_iota(jnp.int32, (new_count, new_count), 1)
    near_ok = near_lane <= near_row
    near_dist = (near_row - near_lane).astype(jnp.float32)
    score_scale = HEAD_DIM ** -0.5

    for d in peers:
        table_copy(d, d).wait_recv()
    to_smem = pltpu.make_async_copy(tbl_recv, tbl_smem, local_sem.at[0])
    to_smem.start()
    for load in loads[:3]:
        load.wait()
    to_smem.wait()

    def wanted_slot(d):
        def step(j, slot):
            entry = tbl_smem[d, 0, j]
            hit = (entry >= 0) & (lax.div(entry, slots) == me)
            return jnp.where(hit, lax.rem(entry, slots), slot)
        slot = jnp.int32(0)
        if max_blocks <= 8:
            for j in range(max_blocks):
                slot = step(j, slot)
            return slot
        return lax.fori_loop(0, max_blocks, step, slot)

    def key_copy(c, d, s):
        return pltpu.make_async_remote_copy(
            src_ref=k_send.at[c, d], dst_ref=k_recv.at[c, s],
            send_sem=k_ss.at[c, d], recv_sem=k_rs.at[c, s],
            device_id={"pool": d}, device_id_type=MESH)

    def value_copy(c, d, s):
        return pltpu.make_async_remote_copy(
            src_ref=v_send.at[c, d], dst_ref=v_recv.at[c, s],
            send_sem=v_ss.at[c, d], recv_sem=v_rs.at[c, s],
            device_id={"pool": d}, device_id_type=MESH)

    wanted = [wanted_slot(d) for d in peers]
    own = wanted_slot(me)

    def send_keys(c):
        part = slice(c * CHUNK, (c + 1) * CHUNK)
        for d, slot in zip(peers, wanted):
            k_send[c, d] = pool_ref[slot, 0, :, part]
            key_copy(c, d, me).start()
        k_recv[c, me] = pool_ref[own, 0, :, part]

    def send_values(c):
        part = slice(c * CHUNK, (c + 1) * CHUNK)
        for d, slot in zip(peers, wanted):
            v_send[c, d] = pool_ref[slot, 1, :, part]
            value_copy(c, d, me).start()
        v_recv[c, me] = pool_ref[own, 1, :, part]

    contract_lanes = (((1,), (1,)), ((), ()))

    def weigh(c):
        for d in peers:
            key_copy(c, d, d).wait_recv()
        for h in range(HEAD_GROUP):
            head = c * HEAD_GROUP + h
            first, width = head_window(h)
            window = slice(c * CHUNK + first, c * CHUNK + first + width)
            slope = jnp.float32(0)
            for t in range(tensors):
                order = ALL_HEADS - HEADS + t * heads_here + head + 1
                slope = jnp.where(core == t, jnp.float32(2.0 ** (-8.0 * order / ALL_HEADS)), slope)
            q_lane = lax.broadcasted_iota(jnp.int32, (new_count, width), 1) + first
            inside = (q_lane >= h * HEAD_DIM) & (q_lane < (h + 1) * HEAD_DIM)
            query = jnp.where(inside, q_ref[0, :, window].astype(jnp.float32), 0.0).astype(jnp.bfloat16)
            far_keys = k_recv[c, :, :, first:first + width].reshape(keys, width)
            far = lax.dot_general(query, far_keys, contract_lanes, preferred_element_type=jnp.float32)
            near = lax.dot_general(query, new_ref[0, 0, :, window], contract_lanes, preferred_element_type=jnp.float32)
            far = jnp.where(far_ok, far * score_scale - slope * far_dist, masked_fill)
            near = jnp.where(near_ok, near * score_scale - slope * near_dist, masked_fill)
            top = jnp.maximum(jnp.max(far, axis=1, keepdims=True), jnp.max(near, axis=1, keepdims=True))
            far = jnp.where(far_ok, jnp.exp(far - top), 0.0).astype(jnp.bfloat16)
            near = jnp.where(near_ok, jnp.exp(near - top), 0.0).astype(jnp.bfloat16)
            total = (jnp.sum(far.astype(jnp.float32), axis=1, keepdims=True)
                     + jnp.sum(near.astype(jnp.float32), axis=1, keepdims=True))
            p_far[head] = far
            p_near[head] = near
            inv_sum[head] = jnp.broadcast_to(1.0 / total, (new_count, LANES))

    def line_copy(c, way, origin):
        block = origin * depth + side
        goal = lax.rem(place + (line - 1 if way else 1), line) * depth + side
        return pltpu.make_async_remote_copy(
            src_ref=ctx.at[block, c], dst_ref=ctx.at[block, c],
            send_sem=line_ss.at[c, way, origin], recv_sem=line_rs.at[c, origin],
            device_id={"pool": goal}, device_id_type=MESH)

    def side_copy(c, origin, at_side):
        block = origin * depth + at_side
        return pltpu.make_async_remote_copy(
            src_ref=ctx.at[block, c], dst_ref=ctx.at[block, c],
            send_sem=side_ss.at[c, origin], recv_sem=side_rs.at[c, origin],
            device_id={"pool": place * depth + (depth - 1 - side)}, device_id_type=MESH)

    def goes_on(way):
        return place >= 1 if way else place < line - 1

    def spread(c, way, origin):
        @pl.when(goes_on(way))
        def _():
            line_copy(c, way, origin).start()

    def pass_on(c, k):
        for way in range(2):
            origin = place + k if way else place - k

            @pl.when(origin < line if way else origin >= 0)
            def _():
                line_copy(c, way, origin).wait_recv()
                spread(c, way, origin)
                if depth == 2:
                    side_copy(c, origin, side).start()

    def attend(c):
        for d in peers:
            value_copy(c, d, d).wait_recv()
        before = None
        tiles = []
        for h in range(HEAD_GROUP):
            head = c * HEAD_GROUP + h
            first, width = head_window(h)
            far_values = v_recv[c, :, :, first:first + width].reshape(keys, width)
            near_values = new_ref[0, 1, :, c * CHUNK + first:c * CHUNK + first + width]
            acc = (jnp.dot(p_far[head], far_values, preferred_element_type=jnp.float32)
                   + jnp.dot(p_near[head], near_values, preferred_element_type=jnp.float32))
            scale = inv_sum[head]
            begin = acc[:, :LANES] * scale
            if before is not None:
                bound = h * HEAD_DIM - first
                tile_lane = lax.broadcasted_iota(jnp.int32, (new_count, LANES), 1)
                tiles.append(jnp.where(tile_lane < bound, before, begin))
            before = begin if width == LANES else acc[:, LANES:] * scale
        for i, tile in enumerate(tiles):
            ctx[me, c, :, i * LANES:(i + 1) * LANES] = tile.astype(jnp.bfloat16)
        for way in range(2):
            spread(c, way, place)
        if depth == 2:
            side_copy(c, place, side).start()

    def all_there(c):
        if depth == 2:
            for origin in range(line):
                side_copy(c, origin, depth - 1 - side).wait_recv()

    pieces = 2 if half % 2 == 0 else 1
    piece = half // pieces

    def term(c, part, i):
        rows = ctx[pl.ds(part * half + i * piece, piece), c].reshape(piece * new_count, CHUNK)
        return jnp.dot(rows, w_ref[c * CHUNK:(c + 1) * CHUNK, :], preferred_element_type=jnp.float32)

    def partial_copy(i):
        return pltpu.make_async_remote_copy(
            src_ref=partial_send.at[i], dst_ref=partial_recv.at[i],
            send_sem=part_ss.at[i], recv_sem=part_rs.at[i],
            device_id={"tensor": other_core}, device_id_type=MESH)

    send_keys(0)
    send_values(0)
    for c in range(1, chunks):
        send_keys(c)
    weigh(0)
    for c in range(chunks):
        last = c == chunks - 1
        attend(c)
        if not last:
            send_values(c + 1)
            weigh(c + 1)
        if c:
            for k in range(line - 1, line):
                pass_on(c - 1, k)
            all_there(c - 1)
            if c == 1:
                loads[3].wait()
            for to, part in ((away, other_core), (kept, core)):
                for i in range(pieces):
                    to[i] = term(c - 1, part, i) if c == 1 else to[i] + term(c - 1, part, i)
        for k in range(1, line if last else line - 1):
            pass_on(c, k)
    all_there(chunks - 1)
    for i in range(pieces):
        partial_send[i] = (away[i] + term(chunks - 1, other_core, i)).astype(jnp.bfloat16)
        partial_copy(i).start()
    for i in range(pieces):
        kept[i] = kept[i] + term(chunks - 1, core, i)
    size = piece * new_count
    for i in range(pieces):
        partial_copy(i).wait_recv()
        out_ref[i * size:(i + 1) * size, :] = (
            kept[i] + partial_recv[i].astype(jnp.float32)).astype(jnp.bfloat16)

    for d in peers:
        table_copy(d, me).wait_send()
        for c in range(chunks):
            key_copy(c, d, me).wait_send()
            value_copy(c, d, me).wait_send()
    for c in range(chunks):
        for origin in range(line):
            for way in range(2):
                @pl.when(goes_on(way) & (origin >= place if way else origin <= place))
                def _():
                    line_copy(c, way, origin).wait_send()
            if depth == 2:
                side_copy(c, origin, side).wait_send()
    for i in range(pieces):
        partial_copy(i).wait_send()


def on_device(owners, tensors, queries, new_kv, kv_pool, block_table, prefix_len, out_weight):
    n = owners
    new_count, head_cols = queries.shape[1:]
    block_len = kv_pool.shape[2]
    columns = out_weight.shape[1]
    chunks = head_cols // CHUNK
    heads_here = chunks * HEAD_GROUP
    half = n // tensors
    depth = 2 if n <= 8 else 1
    line = n // depth
    pieces = 2 if half % 2 == 0 else 1
    size = half // pieces * new_count
    bf16, f32 = jnp.bfloat16, jnp.float32
    vmem = pl.BlockSpec(memory_space=pltpu.VMEM)
    smem = pl.BlockSpec(memory_space=pltpu.SMEM)
    anywhere = pl.BlockSpec(memory_space=pl.ANY)
    dma = pltpu.SemaphoreType.DMA
    blocks = pltpu.VMEM((chunks, n, block_len, CHUNK), bf16)
    return pl.pallas_call(
        functools.partial(kernel, owners, tensors, depth),
        out_shape=jax.ShapeDtypeStruct((half * new_count, columns), bf16),
        in_specs=[smem, smem, vmem, anywhere, anywhere, anywhere, anywhere],
        out_specs=vmem,
        scratch_shapes=[
            pltpu.VMEM(queries.shape, bf16),
            pltpu.VMEM(new_kv.shape, bf16),
            pltpu.VMEM(kv_pool.shape, bf16),
            pltpu.VMEM(out_weight.shape, bf16),
            pltpu.VMEM((8, LANES), jnp.int32),
            pltpu.VMEM((n, 8, LANES), jnp.int32),
            pltpu.SMEM((n, 8, LANES), jnp.int32),
            blocks, blocks, blocks, blocks,
            pltpu.VMEM((heads_here, new_count, n * block_len), bf16),
            pltpu.VMEM((heads_here, new_count, new_count), bf16),
            pltpu.VMEM((heads_here, new_count, LANES), f32),
            pltpu.VMEM((n, chunks, new_count, CHUNK), bf16),
            pltpu.VMEM((pieces, size, columns), f32),
            pltpu.VMEM((pieces, size, columns), f32),
            pltpu.VMEM((pieces, size, columns), bf16),
            pltpu.VMEM((pieces, size, columns), bf16),
            dma((n,)), dma((n,)),
            dma((chunks, n)), dma((chunks, n)), dma((chunks, n)), dma((chunks, n)),
            dma((chunks, 2, line)), dma((chunks, line)),
            dma((chunks, line)), dma((chunks, line)),
            dma((pieces,)), dma((pieces,)), dma((5,)),
        ],
        compiler_params=pltpu.CompilerParams(
            collective_id=0, has_side_effects=True, vmem_limit_bytes=60 << 20),
    )(block_table, prefix_len, block_table, queries, new_kv, kv_pool, out_weight)


def solution(mesh):
    placed = (
        P(("groups", "pool"), None, "tensor"),
        P(("groups", "pool"), None, None, "tensor"),
        P(("groups", "pool"), None, None, "tensor"),
        P(("groups", "pool"), None),
        P(("groups", "pool")),
        P("tensor", "pool"),
    )
    return jax.shard_map(
        functools.partial(on_device, mesh.shape["pool"], mesh.shape["tensor"]),
        mesh=mesh,
        in_specs=placed,
        out_specs=P(("groups", "tensor"), "pool"),
        check_vma=False,
    )
```

time: 78.5 us -> 79.7 us (1.015)
  Pallas kernels: 75.8 us -> 77 us
    pallas_call x1, Pallas kernels: 75.8 us -> 77 us  [on_device(): pl.pallas_call(functools.partial(kernel, owners, tensors, depth), out_sha...]
where the time goes in v2:
time: 79.7 us; the launch traced here: 79.5 us
  Pallas kernels  77 us (97%)
  local copies, waits for them, and re-layouts  1.82 us (2%)
    pallas_call x1, Pallas kernels, on_device(): pl.pallas_call(functools.partial(kernel, owners, tensors, depth), out_sha...  77 us
    unnamed x1, local copies, waits for them, and re-layouts  1.82 us

profile of v2, /device:TPU:0, one launch (start us, length us, event | category | flops | bytes accessed | tf_op | source)
XLA Modules:
  0.0 79.5 jit_solution(17941365922597581397)
XLA Ops:
  0.7 77.0 %shard_map.64 = bf16[256,896]{1,0:T(8,128)(2,1)} custom-call(s32[1,8]{1,0:T(1,128)} %table_v.1, s32[1]{0:T(128)S(6)} %copy.8.length_s, s32[1,8]{1,0:T(1,128)} %table_v.1, bf16[1,64,1792]{2,1,0:T(8,128)(2,1)} %q_hbm.1, bf16[1,2,64,1792]{3,2,1,0:T(8,128)(2,1)} %new_hbm.1, bf16[8,2,32,1792]{3,2,1,0:T(8,128)(2,1)} %pool_hbm.1, bf16[1792,896]{1,0:T(8,128)(2,1)} %w_hbm.1), custom_call_target="tpu_custom_call" | custom-call | tf_op jit(solution)/shard_map/pallas_call | solution.py:324
  77.7 1.8 %copy.9 = bf16[256,896]{1,0:T(8,128)(2,1)} copy(bf16[256,896]{1,0:T(8,128)(2,1)} %shard_map.64) | data formatting | bytes 917504

commit v3 on v1

--- a/solution.py
+++ b/solution.py
@@ -28,11 +28,12 @@
 
 def kernel(
     owners, tensors, zigzag,
-    table_s, length_s, table_v, q_ref, new_ref, pool_ref, w_hbm,
+    table_s, length_s, table_v, q_hbm, new_hbm, pool_hbm, w_hbm,
     out_ref,
+    q_ref, new_ref, pool_ref, q_mate, stat_own, stat_send, stat_recv, acc_send, acc_recv,
     tbl_send, tbl_recv, tbl_smem, k_send, v_send, k_recv, v_recv,
-    p_far, p_near, inv_sum, ctx, w_ref, kept, partial_send, partial_recv,
-    tbl_ss, tbl_rs, k_ss, k_rs, v_ss, v_rs, ring_ss, ring_rs, part_ss, part_rs, local_sem,
+    p_far, p_near, ctx, w_ref, kept, partial_send, partial_recv,
+    tbl_ss, tbl_rs, k_ss, k_rs, v_ss, v_rs, ring_ss, ring_rs, part_ss, part_rs, mate_ss, mate_rs, local_sem,
 ):
     n = owners
     hops = n // 2
@@ -45,8 +46,16 @@
     max_blocks = table_v.shape[1]
     chunks = q_ref.shape[2] // CHUNK
     heads_here = chunks * HEAD_GROUP
-    keys = n * block_len
-
+    near_n = n // 2
+    keys = near_n * block_len
+    base = me // near_n * near_n
+    mate = lax.rem(me + near_n, n)
+    convs = (me, mate)
+
+    loads = [pltpu.make_async_copy(src, dst, local_sem.at[i + 2]) for i, (src, dst) in enumerate(
+        ((q_hbm, q_ref), (pool_hbm, pool_ref), (new_hbm, new_ref)))]
+    for load in loads:
+        load.start()
     w_copy = pltpu.make_async_copy(w_hbm, w_ref, local_sem.at[0])
     w_copy.start()
 
@@ -57,7 +66,8 @@
         pl.semaphore_signal(barrier, inc=1, device_id={"pool": d}, device_id_type=MESH)
     pl.semaphore_signal(barrier, inc=1, device_id={"tensor": other_core}, device_id_type=MESH)
 
-    tbl_send[...] = jnp.zeros_like(tbl_send)
+    length = length_s[0]
+    tbl_send[...] = jnp.full(tbl_send.shape, length, jnp.int32)
     tbl_send[0:1, 0:max_blocks] = table_v[...]
     pl.semaphore_wait(barrier, n)
 
@@ -70,10 +80,23 @@
     for d in peers:
         table_copy(d, me).start()
     tbl_recv[me] = tbl_send[...]
+
+    def mate_copy(i, src, dst):
+        return pltpu.make_async_remote_copy(
+            src_ref=src, dst_ref=dst, send_sem=mate_ss.at[i], recv_sem=mate_rs.at[i],
+            device_id={"pool": mate}, device_id_type=MESH)
+
+    query_copy = mate_copy(0, q_ref, q_mate)
+    stat_copy = mate_copy(1, stat_send, stat_recv)
+    acc_copy = mate_copy(2, acc_send, acc_recv)
+    loads[0].wait()
+    query_copy.start()
     for d in peers:
         table_copy(d, d).wait_recv()
     to_smem = pltpu.make_async_copy(tbl_recv, tbl_smem, local_sem.at[1])
     to_smem.start()
+    loads[1].wait()
+    loads[2].wait()
     to_smem.wait()
 
     def wanted_slot(d):
@@ -88,56 +111,61 @@
             return slot
         return lax.fori_loop(0, max_blocks, step, slot)
 
-    def key_copy(d, s):
-        return pltpu.make_async_remote_copy(
-            src_ref=k_send.at[d], dst_ref=k_recv.at[s],
-            send_sem=k_ss.at[d], recv_sem=k_rs.at[s],
-            device_id={"pool": d}, device_id_type=MESH)
-
-    def value_copy(c, d, s):
-        return pltpu.make_async_remote_copy(
-            src_ref=v_send.at[c, d], dst_ref=v_recv.at[c, s],
-            send_sem=v_ss.at[c, d], recv_sem=v_rs.at[c, s],
-            device_id={"pool": d}, device_id_type=MESH)
-
-    wanted = [wanted_slot(d) for d in peers]
-    for d, slot in zip(peers, wanted):
-        k_send[d] = pool_ref[slot, 0]
-        key_copy(d, me).start()
-    for c in range(chunks):
-        for d, slot in zip(peers, wanted):
-            v_send[c, d] = pool_ref[slot, 1, :, c * CHUNK:(c + 1) * CHUNK]
-            value_copy(c, d, me).start()
-    own = wanted_slot(me)
-    k_recv[me] = pool_ref[own, 0]
-    for c in range(chunks):
-        v_recv[c, me] = pool_ref[own, 1, :, c * CHUNK:(c + 1) * CHUNK]
-
-    length = length_s[0]
+    def key_copy(which, d, s):
+        return pltpu.make_async_remote_copy(
+            src_ref=k_send.at[which, d], dst_ref=k_recv.at[which, s],
+            send_sem=k_ss.at[which, d], recv_sem=k_rs.at[which, s],
+            device_id={"pool": base + d}, device_id_type=MESH)
+
+    def value_copy(which, d, s):
+        return pltpu.make_async_remote_copy(
+            src_ref=v_send.at[which, d], dst_ref=v_recv.at[which, s],
+            send_sem=v_ss.at[which, d], recv_sem=v_rs.at[which, s],
+            device_id={"pool": base + d}, device_id_type=MESH)
+
+    here = me - base
+    near_peers = [lax.rem(here + off, near_n) for off in range(1, near_n)]
+    wanted = [[wanted_slot(lax.rem(base + which * near_n + d, n)) for d in near_peers] for which in range(2)]
+    own = [wanted_slot(conv) for conv in convs]
+    for which in (1, 0):
+        for d, slot in zip(near_peers, wanted[which]):
+            k_send[which, d] = pool_ref[slot, 0]
+            key_copy(which, d, here).start()
+    for which in (1, 0):
+        for d, slot in zip(near_peers, wanted[which]):
+            v_send[which, d] = pool_ref[slot, 1]
+            value_copy(which, d, here).start()
+    for which in range(2):
+        k_recv[which, here] = pool_ref[own[which], 0]
+        v_recv[which, here] = pool_ref[own[which], 1]
+
     lane = lax.broadcasted_iota(jnp.int32, (new_count, keys), 1)
     row = lax.broadcasted_iota(jnp.int32, (new_count, keys), 0)
-    source = lane // block_len
-    offset = lane - source * block_len
-    key_pos = jnp.full((new_count, keys), far_away, jnp.int32)
-    for j in range(max_blocks):
-        entry = table_s[0, j]
-        owner = jnp.where(entry >= 0, lax.div(entry, slots), -1)
-        key_pos = jnp.where(source == owner, j * block_len + offset, key_pos)
-    far_ok = key_pos < length
-    far_dist = (length + row - key_pos).astype(jnp.float32)
+    source = base + lane // block_len
+    offset = lax.rem(lane, block_len)
     near_row = lax.broadcasted_iota(jnp.int32, (new_count, new_count), 0)
     near_lane = lax.broadcasted_iota(jnp.int32, (new_count, new_count), 1)
     near_ok = near_lane <= near_row
     near_dist = (near_row - near_lane).astype(jnp.float32)
     score_scale = HEAD_DIM ** -0.5
-
-    for d in peers:
-        key_copy(d, d).wait_recv()
-
     contract_lanes = (((1,), (1,)), ((), ()))
-    for c in range(chunks):
-        for h in range(HEAD_GROUP):
-            head = c * HEAD_GROUP + h
+    stat_lane = lax.broadcasted_iota(jnp.int32, (new_count, LANES), 1)
+
+    def weigh(which):
+        conv = convs[which]
+        queries = (q_ref, q_mate)[which]
+        conv_length = tbl_smem[conv, 1, 0]
+        key_pos = jnp.full((new_count, keys), far_away, jnp.int32)
+        for j in range(max_blocks):
+            entry = tbl_smem[conv, 0, j]
+            owner = jnp.where(entry >= 0, lax.div(entry, slots), -1)
+            key_pos = jnp.where(source == owner, j * block_len + offset, key_pos)
+        far_ok = key_pos < conv_length
+        far_dist = (conv_length + row - key_pos).astype(jnp.float32)
+        tops = jnp.zeros((new_count, LANES), jnp.float32)
+        totals = jnp.ones((new_count, LANES), jnp.float32)
+        for head in range(heads_here):
+            c, h = divmod(head, HEAD_GROUP)
             first, width = head_window(h)
             window = slice(c * CHUNK + first, c * CHUNK + first + width)
             slope = jnp.float32(0)
@@ -146,20 +174,60 @@
                 slope = jnp.where(core == t, jnp.float32(2.0 ** (-8.0 * order / ALL_HEADS)), slope)
             q_lane = lax.broadcasted_iota(jnp.int32, (new_count, width), 1) + first
             inside = (q_lane >= h * HEAD_DIM) & (q_lane < (h + 1) * HEAD_DIM)
-            query = jnp.where(inside, q_ref[0, :, window].astype(jnp.float32), 0.0).astype(jnp.bfloat16)
-            far_keys = k_recv[:, :, window].reshape(keys, width)
+            query = jnp.where(inside, queries[0, :, window].astype(jnp.float32), 0.0).astype(jnp.bfloat16)
+            far_keys = k_recv[which, :, :, window].reshape(keys, width)
             far = lax.dot_general(query, far_keys, contract_lanes, preferred_element_type=jnp.float32)
-            near = lax.dot_general(query, new_ref[0, 0, :, window], contract_lanes, preferred_element_type=jnp.float32)
             far = jnp.where(far_ok, far * score_scale - slope * far_dist, masked_fill)
-            near = jnp.where(near_ok, near * score_scale - slope * near_dist, masked_fill)
-            top = jnp.maximum(jnp.max(far, axis=1, keepdims=True), jnp.max(near, axis=1, keepdims=True))
+            top = jnp.max(far, axis=1, keepdims=True)
+            if which == 0:
+                near = lax.dot_general(query, new_ref[0, 0, :, window], contract_lanes, preferred_element_type=jnp.float32)
+                near = jnp.where(near_ok, near * score_scale - slope * near_dist, masked_fill)
+                top = jnp.maximum(top, jnp.max(near, axis=1, keepdims=True))
             far = jnp.where(far_ok, jnp.exp(far - top), 0.0).astype(jnp.bfloat16)
-            near = jnp.where(near_ok, jnp.exp(near - top), 0.0).astype(jnp.bfloat16)
-            total = (jnp.sum(far.astype(jnp.float32), axis=1, keepdims=True)
-                     + jnp.sum(near.astype(jnp.float32), axis=1, keepdims=True))
-            p_far[head] = far
-            p_near[head] = near
-            inv_sum[head] = jnp.broadcast_to(1.0 / total, (new_count, LANES))
+            total = jnp.sum(far.astype(jnp.float32), axis=1, keepdims=True)
+            p_far[which, head] = far
+            if which == 0:
+                near = jnp.where(near_ok, jnp.exp(near - top), 0.0).astype(jnp.bfloat16)
+                total = total + jnp.sum(near.astype(jnp.float32), axis=1, keepdims=True)
+                p_near[head] = near
+            tops = jnp.where(stat_lane == head, top, tops)
+            totals = jnp.where(stat_lane == head, total, totals)
+        stat = (stat_own, stat_send)[which]
+        stat[0] = tops
+        stat[1] = totals
+
+    def weighted(which, head):
+        c, h = divmod(head, HEAD_GROUP)
+        first, width = head_window(h)
+        window = slice(c * CHUNK + first, c * CHUNK + first + width)
+        acc = jnp.dot(p_far[which, head], v_recv[which, :, :, window].reshape(keys, width),
+                      preferred_element_type=jnp.float32)
+        if which == 0:
+            acc = acc + jnp.dot(p_near[head], new_ref[0, 1, :, window], preferred_element_type=jnp.float32)
+        return acc
+
+    def joined(c, parts):
+        tiles = []
+        for h in range(1, HEAD_GROUP):
+            bound = h * HEAD_DIM - head_window(h)[0]
+            tiles.append(jnp.where(stat_lane < bound, parts[h - 1][:, -LANES:], parts[h][:, :LANES]))
+        return tiles
+
+    query_copy.wait_recv()
+    for d in near_peers:
+        key_copy(1, d, d).wait_recv()
+    weigh(1)
+    stat_copy.start()
+    for d in near_peers:
+        key_copy(0, d, d).wait_recv()
+    weigh(0)
+    for d in near_peers:
+        value_copy(1, d, d).wait_recv()
+    for c in range(chunks):
+        tiles = joined(c, [weighted(1, c * HEAD_GROUP + h) for h in range(HEAD_GROUP)])
+        for i, tile in enumerate(tiles):
+            acc_send[:, c * CHUNK + i * LANES:c * CHUNK + (i + 1) * LANES] = tile.astype(jnp.bfloat16)
+    acc_copy.start()
 
     def index_at(place):
         if not zigzag:
@@ -186,26 +254,26 @@
             send_sem=ring_ss.at[way, c, k - 1], recv_sem=ring_rs.at[way, c, k - 1],
             device_id={"pool": left if way else right}, device_id_type=MESH)
 
+    for d in near_peers:
+        value_copy(0, d, d).wait_recv()
+    stat_copy.wait_recv()
+    top = jnp.maximum(stat_own[0], stat_recv[0])
+    own_part = jnp.exp(stat_own[0] - top)
+    mate_part = jnp.exp(stat_recv[0] - top)
+    total = own_part * stat_own[1] + mate_part * stat_recv[1]
+    own_part = own_part / total
+    mate_part = mate_part / total
     for c in range(chunks):
-        for d in peers:
-            value_copy(c, d, d).wait_recv()
-        before = None
-        tiles = []
+        parts, others = [], []
         for h in range(HEAD_GROUP):
             head = c * HEAD_GROUP + h
-            first, width = head_window(h)
-            far_values = v_recv[c, :, :, first:first + width].reshape(keys, width)
-            near_values = new_ref[0, 1, :, c * CHUNK + first:c * CHUNK + first + width]
-            acc = (jnp.dot(p_far[head], far_values, preferred_element_type=jnp.float32)
-                   + jnp.dot(p_near[head], near_values, preferred_element_type=jnp.float32))
-            scale = inv_sum[head]
-            begin = acc[:, :LANES] * scale
-            if before is not None:
-                bound = h * HEAD_DIM - first
-                tile_lane = lax.broadcasted_iota(jnp.int32, (new_count, LANES), 1)
-                tiles.append(jnp.where(tile_lane < bound, before, begin))
-            before = begin if width == LANES else acc[:, LANES:] * scale
-        for i, tile in enumerate(tiles):
+            parts.append(weighted(0, head) * own_part[:, head:head + 1])
+            others.append(jnp.broadcast_to(mate_part[:, head:head + 1], (new_count, LANES)))
+        if c == 0:
+            acc_copy.wait_recv()
+        for i, (tile, scale) in enumerate(zip(joined(c, parts), joined(c, others))):
+            lanes = slice(c * CHUNK + i * LANES, c * CHUNK + (i + 1) * LANES)
+            tile = tile + acc_recv[:, lanes].astype(jnp.float32) * scale
             ctx[me, c, :, i * LANES:(i + 1) * LANES] = tile.astype(jnp.bfloat16)
         for way in range(2):
             if travels(way, c, 1):
@@ -256,9 +324,12 @@
 
     for d in peers:
         table_copy(d, me).wait_send()
-        key_copy(d, me).wait_send()
-        for c in range(chunks):
-            value_copy(c, d, me).wait_send()
+    for which in range(2):
+        for d in near_peers:
+            key_copy(which, d, here).wait_send()
+            value_copy(which, d, here).wait_send()
+    for copy in (query_copy, stat_copy, acc_copy):
+        copy.wait_send()
     for k in range(1, hops + 1):
         for c in range(chunks):
             for way in range(2):
@@ -281,31 +352,37 @@
     vmem = pl.BlockSpec(memory_space=pltpu.VMEM)
     smem = pl.BlockSpec(memory_space=pltpu.SMEM)
     dma = pltpu.SemaphoreType.DMA
+    blocks = pltpu.VMEM((2, n // 2, block_len, head_cols), bf16)
     return pl.pallas_call(
         functools.partial(kernel, owners, tensors, owners <= 8),
         out_shape=jax.ShapeDtypeStruct((half * new_count, columns), bf16),
-        in_specs=[smem, smem, vmem, vmem, vmem, vmem, pl.BlockSpec(memory_space=pl.ANY)],
+        in_specs=[smem, smem, vmem] + [pl.BlockSpec(memory_space=pl.ANY)] * 4,
         out_specs=vmem,
         scratch_shapes=[
+            pltpu.VMEM(queries.shape, bf16),
+            pltpu.VMEM(new_kv.shape, bf16),
+            pltpu.VMEM(kv_pool.shape, bf16),
+            pltpu.VMEM(queries.shape, bf16),
+            pltpu.VMEM((2, new_count, LANES), f32),
+            pltpu.VMEM((2, new_count, LANES), f32),
+            pltpu.VMEM((2, new_count, LANES), f32),
+            pltpu.VMEM((new_count, head_cols), bf16),
+            pltpu.VMEM((new_count, head_cols), bf16),
             pltpu.VMEM((8, LANES), jnp.int32),
             pltpu.VMEM((n, 8, LANES), jnp.int32),
             pltpu.SMEM((n, 8, LANES), jnp.int32),
-            pltpu.VMEM((n, block_len, head_cols), bf16),
-            pltpu.VMEM((chunks, n, block_len, CHUNK), bf16),
-            pltpu.VMEM((n, block_len, head_cols), bf16),
-            pltpu.VMEM((chunks, n, block_len, CHUNK), bf16),
-            pltpu.VMEM((heads_here, new_count, n * block_len), bf16),
+            blocks, blocks, blocks, blocks,
+            pltpu.VMEM((2, heads_here, new_count, n // 2 * block_len), bf16),
             pltpu.VMEM((heads_here, new_count, new_count), bf16),
-            pltpu.VMEM((heads_here, new_count, LANES), f32),
             pltpu.VMEM((n, chunks, new_count, CHUNK), bf16),
             pltpu.VMEM((head_cols, columns), bf16),
             pltpu.VMEM((half, new_count, columns), f32),
             pltpu.VMEM((half, new_count, columns), bf16),
             pltpu.VMEM((half, new_count, columns), bf16),
-            dma((n,)), dma((n,)), dma((n,)), dma((n,)),
-            dma((chunks, n)), dma((chunks, n)),
+            dma((n,)), dma((n,)),
+            dma((2, n // 2)), dma((2, n // 2)), dma((2, n // 2)), dma((2, n // 2)),
             dma((2, chunks, hops)), dma((2, chunks, hops)),
-            dma((half,)), dma((half,)), dma((2,)),
+            dma((half,)), dma((half,)), dma((3,)), dma((3,)), dma((5,)),
         ],
         compiler_params=pltpu.CompilerParams(
             collective_id=0, has_side_effects=True, vmem_limit_bytes=60 << 20),

time: 78.5 us -> 73.1 us (0.931)
  Pallas kernels: 75.8 us -> 70.4 us
    pallas_call x1, Pallas kernels: 75.8 us -> 70.4 us  [on_device(): pl.pallas_call(functools.partial(kernel, owners, tensors, owners <= 8), o...]
where the time goes in v3:
time: 73.1 us; the launch traced here: 72.9 us
  Pallas kernels  70.4 us (96%)
  local copies, waits for them, and re-layouts  1.82 us (2%)
    pallas_call x1, Pallas kernels, on_device(): pl.pallas_call(functools.partial(kernel, owners, tensors, owners <= 8), o...  70.4 us
    unnamed x1, local copies, waits for them, and re-layouts  1.82 us

profile of v3, /device:TPU:0, one launch (start us, length us, event | category | flops | bytes accessed | tf_op | source)
XLA Modules:
  0.0 72.9 jit_solution(4948649269250002078)
XLA Ops:
  0.7 70.4 %shard_map.64 = bf16[256,896]{1,0:T(8,128)(2,1)} custom-call(s32[1,8]{1,0:T(1,128)} %table_v.1, s32[1]{0:T(128)S(6)} %copy.8.length_s, s32[1,8]{1,0:T(1,128)} %table_v.1, bf16[1,64,1792]{2,1,0:T(8,128)(2,1)} %q_hbm.1, bf16[1,2,64,1792]{3,2,1,0:T(8,128)(2,1)} %new_hbm.1, bf16[8,2,32,1792]{3,2,1,0:T(8,128)(2,1)} %pool_hbm.1, bf16[1792,896]{1,0:T(8,128)(2,1)} %w_hbm.1), custom_call_target="tpu_custom_call" | custom-call | tf_op jit(solution)/shard_map/pallas_call | solution.py:356
  71.1 1.8 %copy.9 = bf16[256,896]{1,0:T(8,128)(2,1)} copy(bf16[256,896]{1,0:T(8,128)(2,1)} %shard_map.64) | data formatting | bytes 917504

commit v4 on v3

--- a/solution.py
+++ b/solution.py
@@ -131,7 +131,6 @@
         for d, slot in zip(near_peers, wanted[which]):
             k_send[which, d] = pool_ref[slot, 0]
             key_copy(which, d, here).start()
-    for which in (1, 0):
         for d, slot in zip(near_peers, wanted[which]):
             v_send[which, d] = pool_ref[slot, 1]
             value_copy(which, d, here).start()
@@ -219,15 +218,15 @@
     weigh(1)
     stat_copy.start()
     for d in near_peers:
-        key_copy(0, d, d).wait_recv()
-    weigh(0)
-    for d in near_peers:
         value_copy(1, d, d).wait_recv()
     for c in range(chunks):
         tiles = joined(c, [weighted(1, c * HEAD_GROUP + h) for h in range(HEAD_GROUP)])
         for i, tile in enumerate(tiles):
             acc_send[:, c * CHUNK + i * LANES:c * CHUNK + (i + 1) * LANES] = tile.astype(jnp.bfloat16)
     acc_copy.start()
+    for d in near_peers:
+        key_copy(0, d, d).wait_recv()
+    weigh(0)
 
     def index_at(place):
         if not zigzag:

time: 73.1 us -> 71.1 us (0.973)
  Pallas kernels: 70.4 us -> 68.5 us
    pallas_call x1, Pallas kernels: 70.4 us -> 68.5 us  [on_device(): pl.pallas_call(functools.partial(kernel, owners, tensors, owners <= 8), o...]
where the time goes in v4:
time: 71.1 us; the launch traced here: 71 us
  Pallas kernels  68.5 us (96%)
  local copies, waits for them, and re-layouts  1.82 us (3%)
    pallas_call x1, Pallas kernels, on_device(): pl.pallas_call(functools.partial(kernel, owners, tensors, owners <= 8), o...  68.5 us
    unnamed x1, local copies, waits for them, and re-layouts  1.82 us

profile of v4, /device:TPU:0, one launch (start us, length us, event | category | flops | bytes accessed | tf_op | source)
XLA Modules:
  0.0 71.0 jit_solution(9163043840886618953)
XLA Ops:
  0.7 68.5 %shard_map.64 = bf16[256,896]{1,0:T(8,128)(2,1)} custom-call(s32[1,8]{1,0:T(1,128)} %table_v.1, s32[1]{0:T(128)S(6)} %copy.8.length_s, s32[1,8]{1,0:T(1,128)} %table_v.1, bf16[1,64,1792]{2,1,0:T(8,128)(2,1)} %q_hbm.1, bf16[1,2,64,1792]{3,2,1,0:T(8,128)(2,1)} %new_hbm.1, bf16[8,2,32,1792]{3,2,1,0:T(8,128)(2,1)} %pool_hbm.1, bf16[1792,896]{1,0:T(8,128)(2,1)} %w_hbm.1), custom_call_target="tpu_custom_call" | custom-call | tf_op jit(solution)/shard_map/pallas_call | solution.py:355
  69.2 1.8 %copy.9 = bf16[256,896]{1,0:T(8,128)(2,1)} copy(bf16[256,896]{1,0:T(8,128)(2,1)} %shard_map.64) | data formatting | bytes 917504
